TPU v7x, 32 devices: a whole 2x2x4 slice. The times are simulated.
32 devices in a mesh: groups: 2 (over y), tensor: 4 (over z), dp: 2 (over x), pipe: 2 (over core).
Axes of the slice: x: 2, y: 2, z: 4, core: 2. Of those that a mesh axis runs over, the one named last changes fastest.
Arguments:
- residual_input: bfloat16 [512, 8192], P(('groups', 'dp'), 'tensor'), parts along dimension 0, may hold values from -6 to 6
- norm_gain_layers: float32 [2, 8192], replicated, may hold values from 0.25 to 1.75
- query_projection_weight: bfloat16 [2, 8192, 8192], P('pipe', 'dp', 'tensor'), may hold values from -0.0625 to 0.0625
- output_projection_weight: bfloat16 [2, 8192, 8192], P('pipe', 'tensor', 'dp'), may hold values from -0.0625 to 0.0625
- query_down_maps: bfloat16 [2, 8, 8192, 64], P('pipe', None, None, 'tensor'), may hold values from -0.0625 to 0.0625
- query_up_maps: bfloat16 [2, 8, 64, 8192], P('pipe', None, None, 'tensor'), may hold values from -0.75 to 0.75
- output_down_maps: bfloat16 [2, 8, 8192, 64], P('pipe', None, 'tensor'), may hold values from -0.0625 to 0.0625
- output_up_maps: bfloat16 [2, 8, 64, 8192], P('pipe', None, None, 'tensor'), may hold values from -0.75 to 0.75
- keyval_cache: bfloat16 [2, 512, 8, 16, 256], P('pipe', ('groups', 'dp'), 'tensor'), parts along dimension 1, may hold values from -120 to 120, as said below
- token_keyval: bfloat16 [2, 512, 8, 256], P('pipe', ('groups', 'dp'), 'tensor'), parts along dimension 1, may hold values from -4 to 4, as said below
- row_adapter_index: int32 [512], P(('groups', 'dp')), parts along dimension 0, may hold values from 0 to 7
- cache_length: int32 [512], P(('groups', 'dp')), parts along dimension 0, may hold values from 1 to 16, as said below
Outputs:
- hidden_out: bfloat16 [512, 8192], P(('groups', 'dp', 'pipe'), 'tensor'), parts along dimension 0
There are 2 independent parts, one for each index of `groups`. A program takes and returns all parts, laid end to end along the dimension named above; an argument that names none is the same for every part. Nothing has to cross between parts.
Inputs may be any that keep to these rules, and one draw needn't show every extreme that they name: `cache_length`: some row has all 16 positions valid and some row has one. `keyval_cache`: slot s is a copy of key-value head s * 1: slots of the same key-value head are equal. `token_keyval`: slot s is a copy of key-value head s * 1: slots of the same key-value head are equal.
All inputs are finite; a program needn't handle non-finite values.
Results may differ from a plain program's by a relative error of at most 0.028.
Values may be sent and summed in bfloat16 or wider, within the bound.
A program may use at most 256 MiB of HBM per device.

v0:
```python
import jax
import jax.numpy as jnp
from jax import lax
from jax.sharding import PartitionSpec as P

EPSILON = 1e-05
ADAPTER_SCALE = 2.0


def shifted(block, axis, distance):
    devices = range(lax.axis_size(axis))
    route = [(i - distance, i) for i in devices if i - distance in devices]
    return lax.ppermute(block, axis, route)


def widen_rank(adapter_selector, rank_vec):
    spread = adapter_selector[:, :, None] * rank_vec.astype(jnp.float32)[:, None, :]
    return spread.reshape(spread.shape[0], -1).astype(jnp.bfloat16)


def attend(queries, layer_cache, newest_keyval, row_valid_length):
    head_dim = queries.shape[-1]
    inv_scale = head_dim ** (-0.5)
    cache_keys = layer_cache[..., :head_dim]
    cache_vals = layer_cache[..., head_dim:]
    new_key = newest_keyval[..., :head_dim]
    new_val = newest_keyval[..., head_dim:]
    valid_mask = (
        jnp.arange(layer_cache.shape[2], dtype=jnp.int32)[None, :] < row_valid_length[:, None]
    )[:, None, None, :]
    scores = (
        jnp.einsum("nshd,nsld->nshl", queries, cache_keys, preferred_element_type=jnp.float32)
        * inv_scale
    )
    new_score = (
        jnp.einsum("nshd,nsd->nsh", queries, new_key, preferred_element_type=jnp.float32)
        * inv_scale
    )
    row_max = jnp.maximum(jnp.max(jnp.where(valid_mask, scores, -1e30), axis=-1), new_score)
    exp_cache = jnp.where(valid_mask, jnp.exp(scores - row_max[..., None]), 0.0)
    exp_new = jnp.exp(new_score - row_max)
    totals = jnp.sum(exp_cache, axis=-1) + exp_new
    prob_cache = (exp_cache / totals[..., None]).astype(jnp.bfloat16)
    prob_new = (exp_new / totals).astype(jnp.bfloat16)
    attention_result = jnp.einsum(
        "nshl,nsld->nshd", prob_cache, cache_vals, preferred_element_type=jnp.float32
    )
    attention_result = (
        attention_result
        + prob_new.astype(jnp.float32)[..., None] * new_val.astype(jnp.float32)[:, :, None, :]
    )
    return attention_result.astype(jnp.bfloat16)


def run_layer(
    incoming_state,
    layer_row_gain,
    query_matrix,
    adapter_group,
    row_adapter_picks,
    row_valid_length,
    layer_cache,
    newest_keyval,
    output_pieces,
):
    query_down_picked, query_up_picked, output_down_picked, output_up_picked = adapter_group
    adapters = query_down_picked.shape[0]
    rank = query_up_picked.shape[1]
    micro_rows = incoming_state.shape[0]
    head_dim = layer_cache.shape[-1] // 2
    slot_count = layer_cache.shape[1]
    gathered = lax.all_gather(incoming_state, "tensor", axis=1, tiled=True)
    hidden_single = gathered.astype(jnp.float32)
    mean_sq = jnp.mean(hidden_single * hidden_single, axis=-1, keepdims=True)
    normed_state = (hidden_single * lax.rsqrt(mean_sq + EPSILON) * layer_row_gain).astype(
        jnp.bfloat16
    )
    adapter_selector = (
        row_adapter_picks[:, None] == jnp.arange(adapters, dtype=jnp.int32)[None, :]
    ).astype(jnp.float32)
    rank_every_query = jnp.einsum(
        "iq,gqh->igh", normed_state, query_down_picked, preferred_element_type=jnp.float32
    )
    rank_local = jnp.sum(adapter_selector[:, :, None] * rank_every_query, axis=1).astype(
        jnp.bfloat16
    )
    query_rank_state = lax.all_gather(rank_local, "tensor", axis=1, tiled=True)
    plain_query = jnp.dot(normed_state, query_matrix, preferred_element_type=jnp.float32)
    query_state = plain_query + ADAPTER_SCALE * jnp.dot(
        widen_rank(adapter_selector, query_rank_state),
        query_up_picked.reshape(adapters * rank, -1),
        preferred_element_type=jnp.float32,
    )
    query_state = query_state.astype(jnp.bfloat16).reshape(micro_rows, slot_count, -1, head_dim)
    attention_result = attend(query_state, layer_cache, newest_keyval, row_valid_length).reshape(
        micro_rows, -1
    )
    plain_output = lax.psum_scatter(
        output_pieces(attention_result).astype(jnp.bfloat16),
        "tensor",
        scatter_dimension=1,
        tiled=True,
    ).astype(jnp.float32)
    rank_every_output = jnp.einsum(
        "cb,dbm->cdm", attention_result, output_down_picked, preferred_element_type=jnp.float32
    )
    rank_part = jnp.sum(adapter_selector[:, :, None] * rank_every_output, axis=1)
    output_rank_state = lax.psum(rank_part, "tensor").astype(jnp.bfloat16)
    adapter_result = jnp.dot(
        widen_rank(adapter_selector, output_rank_state),
        output_up_picked.reshape(adapters * rank, -1),
        preferred_element_type=jnp.float32,
    )
    return (
        incoming_state.astype(jnp.float32) + plain_output + ADAPTER_SCALE * adapter_result
    ).astype(jnp.bfloat16)


def body(
    residual_input,
    norm_gain_layers,
    query_projection_weight,
    output_projection_weight,
    query_down_maps,
    query_up_maps,
    output_down_maps,
    output_up_maps,
    keyval_cache,
    token_keyval,
    row_adapter_index,
    cache_length,
):
    section_index = lax.axis_index("pipe")
    micro_rows = residual_input.shape[0] // 2
    layer_groups = (
        query_projection_weight,
        output_projection_weight,
        query_down_maps,
        query_up_maps,
        output_down_maps,
        output_up_maps,
    )
    query_sets = lax.all_gather(layer_groups[0], "dp", axis=1, tiled=True)
    output_full = lax.all_gather(layer_groups[1][0], "dp", axis=1, tiled=True)
    adapter_group = tuple((adapter_member[0] for adapter_member in layer_groups[2:]))
    layer_row_gain = lax.dynamic_index_in_dim(norm_gain_layers, section_index, 0, keepdims=False)

    def output_pieces(attention_result):
        return jnp.dot(attention_result, output_full, preferred_element_type=jnp.float32)

    section_out = jnp.zeros((micro_rows, residual_input.shape[1]), jnp.bfloat16)
    first_out = section_out
    for tick_step in range(3):
        if tick_step > 0:
            passed = shifted(section_out, "pipe", 1)
        else:
            passed = section_out
        micro_block = jnp.clip(tick_step - section_index, 0, 1)
        row_start = micro_block * micro_rows
        own_rows = lax.dynamic_slice_in_dim(residual_input, row_start, micro_rows, 0)
        incoming_state = jnp.where(section_index == 0, own_rows, passed)
        row_adapter_picks = lax.dynamic_slice_in_dim(row_adapter_index, row_start, micro_rows, 0)
        row_valid_length = lax.dynamic_slice_in_dim(cache_length, row_start, micro_rows, 0)
        layer_cache = lax.dynamic_slice_in_dim(keyval_cache[0], row_start, micro_rows, 0)
        newest_keyval = lax.dynamic_slice_in_dim(token_keyval[0], row_start, micro_rows, 0)
        section_out = run_layer(
            incoming_state,
            layer_row_gain,
            query_sets[0],
            adapter_group,
            row_adapter_picks,
            row_valid_length,
            layer_cache,
            newest_keyval,
            output_pieces,
        )
        if tick_step == 1:
            first_out = section_out
    returned = shifted(first_out, "pipe", -1)
    result = jnp.where(section_index == 0, returned, section_out)
    return result


def solution(mesh):
    return jax.shard_map(
        body,
        mesh=mesh,
        in_specs=(
            P(("groups", "dp"), "tensor"),
            P(),
            P("pipe", "dp", "tensor"),
            P("pipe", "tensor", "dp"),
            P("pipe", None, None, "tensor"),
            P("pipe", None, None, "tensor"),
            P("pipe", None, "tensor", None),
            P("pipe", None, None, "tensor"),
            P("pipe", ("groups", "dp"), "tensor", None, None),
            P("pipe", ("groups", "dp"), "tensor", None),
            P(("groups", "dp")),
            P(("groups", "dp")),
        ),
        out_specs=P(("groups", "dp", "pipe"), "tensor"),
        check_vma=False,
    )
```

profile of v0, /device:TPU:1, one launch (start us, length us, event | category | flops | bytes accessed | tf_op | source)
XLA Modules:
  0.0 1098.5 jit_solution(8175694537662737251)
XLA Ops:
  10.9 3.6 dynamic-slice_bitcast_fusion
  15.3 23.6 %all-gather.7.cloned.1.call-done = bf16[64,8192]{1,0:T(8,128)(2,1)} async-done(((bf16[64,2048]{1,0:T(8,128)(2,1)}), bf16[64,8192]{1,0:T(8,128)(2,1)}) %all-gather.7.cloned.1.call-update) | async-done | bytes 1048592 | tf_op jit(solution)/shard_map/all_gather | solution.py:72
  40.4 2.8 fusion.83
  43.2 10.2 all_gather.26
  53.9 374.7 %all-gather.9.cloned.1.call-done = bf16[1,8192,2048]{2,1,0:T(8,128)(2,1)} async-done(((bf16[1,4096,2048]{2,1,0:T(8,128)(2,1)}), bf16[1,8192,2048]{2,1,0:T(8,128)(2,1)}) %all-gather.9.cloned.1.call-update) | async-done | bytes 33554448 | tf_op jit(solution)/shard_map/all_gather | solution.py:143
  428.6 16.1 %fusion.10 = f32[64,2048]{1,0:T(8,128)S(1)} fusion(bf16[1,8192,2048]{2,1,0:T(8,128)(2,1)} %all-gather.9.cloned.1.call-done, bf16[64,8192]{1,0:T(8,128)(2,1)S(1)} %copy-done.1, f32[8192]{0:T(1024)S(1)} %bitcast.193, f32[64]{0:T(128)S(1)} %add_rsqrt_fusion.2), kind=kOutput, calls=%fused_computation.10 | convolution fusion | flops 2149580800 | bytes 35160320 | tf_op jit(solution)/shard_map/dot_general | solution.py:88
  456.8 362.0 %all-gather.15.cloned.1.call-done = bf16[1,2048,8192]{2,1,0:T(8,128)(2,1)} async-done(((bf16[1,2048,4096]{2,1,0:T(8,128)(2,1)}), bf16[1,2048,8192]{2,1,0:T(8,128)(2,1)}) %all-gather.15.cloned.1.call-update) | async-done | bytes 33554448 | tf_op jit(solution)/shard_map/all_gather | solution.py:144
  818.8 14.7 %fusion.12 = bf16[64,8192]{1,0:T(8,128)(2,1)} fusion(bf16[1,2048,8192]{2,1,0:T(8,128)(2,1)} %all-gather.15.cloned.1.call-done, bf16[8,8,16,128]{3,2,1,0:T(8,128)(2,1)S(1)} %bitcast.183), kind=kOutput, calls=%fused_computation.12 | convolution fusion | flops 2148007936 | bytes 34865152 | tf_op jit(solution)/shard_map/dot_general | solution.py:149
  836.4 17.4 %psum.21 = bf16[64,64]{1,0:T(8,128)(2,1)S(1)} all-reduce(f32[64,64]{1,0:T(8,128)S(1)} %fusion.65), channel_id=1, replica_groups=mesh['groups'=2,'tensor'=4,'dp'=2,'pipe'=2] {'tensor'}, use_global_device_ids=true, to_apply=%region_6.7 | all-reduce | flops 4096 | bytes 24576 | tf_op jit(solution)/shard_map/psum | solution.py:108
  854.1 7.2 reduce-scatter.4.cloned.1.call-done
  869.5 24.7 %all-gather.11.cloned.1.call-done = bf16[64,8192]{1,0:T(8,128)(2,1)} async-done(((bf16[64,2048]{1,0:T(8,128)(2,1)}), bf16[64,8192]{1,0:T(8,128)(2,1)}) %all-gather.11.cloned.1.call-update) | async-done | bytes 1048592 | tf_op jit(solution)/shard_map/all_gather | solution.py:72
  895.8 2.8 fusion.80
  898.6 10.2 all_gather.29
  909.3 13.7 %fusion.8 = f32[64,2048]{1,0:T(8,128)S(1)} fusion(bf16[1,8192,2048]{2,1,0:T(8,128)(2,1)} %all-gather.9.cloned.1.call-done, bf16[64,8192]{1,0:T(8,128)(2,1)S(1)} %copy-done.2, f32[64]{0:T(128)S(1)} %add_rsqrt_fusion.1, f32[8192]{0:T(1024)S(1)} %bitcast.195), kind=kOutput, calls=%fused_computation.8 | convolution fusion | flops 2149580800 | bytes 35160320 | tf_op jit(solution)/shard_map/dot_general | solution.py:88
  930.2 14.7 %fusion.15 = bf16[64,8192]{1,0:T(8,128)(2,1)} fusion(bf16[1,2048,8192]{2,1,0:T(8,128)(2,1)} %all-gather.15.cloned.1.call-done, bf16[8,8,16,128]{3,2,1,0:T(8,128)(2,1)S(1)} %bitcast.185), kind=kOutput, calls=%fused_computation.13 | convolution fusion | flops 2148007936 | bytes 34865152 | tf_op jit(solution)/shard_map/dot_general | solution.py:149
  947.8 14.9 %psum.22 = bf16[64,64]{1,0:T(8,128)(2,1)S(1)} all-reduce(f32[64,64]{1,0:T(8,128)S(1)} %fusion.62), channel_id=1, replica_groups=mesh['groups'=2,'tensor'=4,'dp'=2,'pipe'=2] {'tensor'}, use_global_device_ids=true, to_apply=%region_13.14 | all-reduce | flops 4096 | bytes 24576 | tf_op jit(solution)/shard_map/psum | solution.py:108
  963.1 12.2 %reduce-scatter.6.cloned.1.call-done = bf16[64,2048]{1,0:T(8,128)(2,1)} async-done(((bf16[64,8192]{1,0:T(8,128)(2,1)}), bf16[64,2048]{1,0:T(8,128)(2,1)}) %reduce-scatter.6.cloned.1.call-update) | async-done | bytes 262160 | tf_op jit(solution)/shard_map/reduce_scatter | solution.py:98
  981.8 26.4 %all-gather.13.cloned.1.call-done = bf16[64,8192]{1,0:T(8,128)(2,1)} async-done(((bf16[64,2048]{1,0:T(8,128)(2,1)}), bf16[64,8192]{1,0:T(8,128)(2,1)}) %all-gather.13.cloned.1.call-update) | async-done | bytes 1048592 | tf_op jit(solution)/shard_map/all_gather | solution.py:72
  1012.5 10.5 all_gather.31
  1023.5 13.7 %fusion.6 = f32[64,2048]{1,0:T(8,128)S(1)} fusion(bf16[1,8192,2048]{2,1,0:T(8,128)(2,1)} %all-gather.9.cloned.1.call-done, bf16[64,8192]{1,0:T(8,128)(2,1)S(1)} %copy-done.3, f32[64]{0:T(128)S(1)} %add_rsqrt_fusion, f32[8192]{0:T(1024)S(1)} %bitcast.197), kind=kOutput, calls=%fused_computation.6 | convolution fusion | flops 2149580800 | bytes 35160320 | tf_op jit(solution)/shard_map/dot_general | solution.py:88
  1044.4 14.7 %fusion.18 = bf16[64,8192]{1,0:T(8,128)(2,1)} fusion(bf16[1,2048,8192]{2,1,0:T(8,128)(2,1)} %all-gather.15.cloned.1.call-done, bf16[8,8,16,128]{3,2,1,0:T(8,128)(2,1)S(1)} %bitcast.184), kind=kOutput, calls=%fused_computation.14 | convolution fusion | flops 2148007936 | bytes 34865152 | tf_op jit(solution)/shard_map/dot_general | solution.py:149
  1059.1 6.3 collective-permute-start.1
  1068.3 16.2 %psum.23 = bf16[64,64]{1,0:T(8,128)(2,1)S(1)} all-reduce(f32[64,64]{1,0:T(8,128)S(1)} %fusion.59), channel_id=1, replica_groups=mesh['groups'=2,'tensor'=4,'dp'=2,'pipe'=2] {'tensor'}, use_global_device_ids=true, to_apply=%region_20.21 | all-reduce | flops 4096 | bytes 24576 | tf_op jit(solution)/shard_map/psum | solution.py:108
  1087.0 2.8 reduce-scatter.8.cloned.1.call-done
  (163 shorter events, 68.2 us)
Async XLA Ops:
  6.5 438.2 %copy-start = (bf16[1,8,64,2048]{3,2,1,0:T(8,128)(2,1)S(1)}, bf16[1,8,64,2048]{3,2,1,0:T(8,128)(2,1)}, u32[]{:S(2)}) copy-start(bf16[1,8,64,2048]{3,2,1,0:T(8,128)(2,1)} %param.17) | copy-start | bytes 6291460
  6.5 32.3 %all-gather.7.cloned.1.call-start = ((), (), s32[]{:S(2)}) async-start(), calls=%async_computation.3 | async-start | bytes 1310720 | tf_op jit(solution)/shard_map/all_gather | solution.py:72
  8.4 420.2 %all-gather.9.cloned.1.call-start = ((), (), s32[]{:S(2)}) async-start(), calls=%async_computation.4 | async-start | bytes 50331648 | tf_op jit(solution)/shard_map/all_gather | solution.py:143
  9.2 809.6 %all-gather.15.cloned.1.call-start = ((), (), s32[]{:S(2)}) async-start(), calls=%async_computation.10 | async-start | bytes 50331648 | tf_op jit(solution)/shard_map/all_gather | solution.py:144
  9.9 851.4 %reduce-scatter.4.cloned.1.call-start = ((), (), s32[]{:S(2)}) async-start(), calls=%async_computation.5 | async-start | bytes 1310720 | tf_op jit(solution)/shard_map/reduce_scatter | solution.py:98
  10.9 4.4 copy-start.18
  40.4 388.2 %copy-start.1 = (bf16[64,8192]{1,0:T(8,128)(2,1)S(1)}, bf16[64,8192]{1,0:T(8,128)(2,1)}, u32[]{:S(2)}) copy-start(bf16[64,8192]{1,0:T(8,128)(2,1)} %all-gather.7.cloned.1.call-done) | copy-start | bytes 3145732
  451.9 3.2 copy-start.15
  833.5 27.9 %copy-start.4 = (bf16[64,2048]{1,0:T(8,128)(2,1)S(1)}, bf16[64,2048]{1,0:T(8,128)(2,1)}, u32[]{:S(2)}) copy-start(bf16[64,2048]{1,0:T(8,128)(2,1)} %dynamic-slice_select_fusion.1) | copy-start | bytes 786436
  833.5 60.7 %all-gather.11.cloned.1.call-start = ((), (), s32[]{:S(2)}) async-start(), calls=%async_computation.6 | async-start | bytes 1310720 | tf_op jit(solution)/shard_map/all_gather | solution.py:72
  836.4 30.5 %copy-start.10 = (bf16[128,2048]{1,0:T(8,128)(2,1)S(1)}, bf16[128,2048]{1,0:T(8,128)(2,1)}, u32[]{:S(2)}) copy-start(bf16[128,2048]{1,0:T(8,128)(2,1)} %param.12) | copy-start | bytes 1572868
  863.4 3.4 collective-permute-start
  867.6 107.6 %reduce-scatter.6.cloned.1.call-start = ((), (), s32[]{:S(2)}) async-start(), calls=%async_computation.7 | async-start | bytes 1310720 | tf_op jit(solution)/shard_map/reduce_scatter | solution.py:98
  895.8 13.5 %copy-start.2 = (bf16[64,8192]{1,0:T(8,128)(2,1)S(1)}, bf16[64,8192]{1,0:T(8,128)(2,1)}, u32[]{:S(2)}) copy-start(bf16[64,8192]{1,0:T(8,128)(2,1)} %all-gather.11.cloned.1.call-done) | copy-start | bytes 3145732
  944.9 30.4 %copy-start.5 = (bf16[64,2048]{1,0:T(8,128)(2,1)S(1)}, bf16[64,2048]{1,0:T(8,128)(2,1)}, u32[]{:S(2)}) copy-start(bf16[64,2048]{1,0:T(8,128)(2,1)} %dynamic-slice_select_fusion.2) | copy-start | bytes 786436
  944.9 63.2 %all-gather.13.cloned.1.call-start = ((), (), s32[]{:S(2)}) async-start(), calls=%async_computation.8 | async-start | bytes 1310720 | tf_op jit(solution)/shard_map/all_gather | solution.py:72
  947.8 33.0 %copy-start.11 = (bf16[128,2048]{1,0:T(8,128)(2,1)S(1)}, bf16[128,2048]{1,0:T(8,128)(2,1)}, u32[]{:S(2)}) copy-start(bf16[128,2048]{1,0:T(8,128)(2,1)} %param.12) | copy-start | bytes 1572868
  977.4 32.3 %copy-start.13 = (bf16[64,2048]{1,0:T(8,128)(2,1)}, bf16[64,2048]{1,0:T(8,128)(2,1)S(1)}, u32[]{:S(2)}) copy-start(bf16[64,2048]{1,0:T(8,128)(2,1)S(1)} %add_convert_fusion.1) | copy-start | bytes 786436
  977.4 3.4 collective-permute-start.2
  981.6 108.2 %reduce-scatter.8.cloned.1.call-start = ((), (), s32[]{:S(2)}) async-start(), calls=%async_computation.9 | async-start | bytes 1310720 | tf_op jit(solution)/shard_map/reduce_scatter | solution.py:98
  1009.7 13.7 %copy-start.3 = (bf16[64,8192]{1,0:T(8,128)(2,1)S(1)}, bf16[64,8192]{1,0:T(8,128)(2,1)}, u32[]{:S(2)}) copy-start(bf16[64,8192]{1,0:T(8,128)(2,1)} %all-gather.13.cloned.1.call-done) | copy-start | bytes 3145732
  1044.4 14.8 %copy-start.14 = (bf16[64,2048]{1,0:T(8,128)(2,1)S(1)}, bf16[64,2048]{1,0:T(8,128)(2,1)}, u32[]{:S(2)}) copy-start(bf16[64,2048]{1,0:T(8,128)(2,1)} %copy-done.13) | copy-start | bytes 786436
  1059.1 27.8 %collective-permute-start.1 = (bf16[64,2048]{1,0:T(8,128)(2,1)S(1)}, bf16[64,2048]{1,0:T(8,128)(2,1)}, u32[]{:S(2)}, u32[]{:S(2)}) collective-permute-start(bf16[64,2048]{1,0:T(8,128)(2,1)S(1)} %copy-done.14), channel_id=1, source_target_pairs={{1,0},{3,2},{5,4},{7,6},{9,8},{11,10},{13,12},{15,14},{17,16},{19,... | collective-permute-start | bytes 786440 | tf_op jit(solution)/shard_map/ppermute | solution.py:13
  1068.3 21.6 %copy-start.6 = (bf16[64,2048]{1,0:T(8,128)(2,1)S(1)}, bf16[64,2048]{1,0:T(8,128)(2,1)}, u32[]{:S(2)}) copy-start(bf16[64,2048]{1,0:T(8,128)(2,1)} %dynamic-slice_select_fusion) | copy-start | bytes 786436
  (8 other events, 8.2 us)
Sparse Core Ops, SparseCore 0:
  8.9 29.8 all-gather.6
  40.4 388.1 all-gather.8
  430.2 388.5 all-gather.14
  833.6 27.6 reduce-scatter.3
  867.8 26.4 all-gather.10
  945.1 30.1 reduce-scatter.5
  981.7 26.3 all-gather.12
  1059.2 30.5 reduce-scatter.7
where the time goes:
time: 1100 us
  waiting for transfers between devices  839 us (76%)
  matrix products  123 us (11%)
  blocking collectives  79.4 us (7%)
  other arithmetic  17.6 us (2%)
  local copies, waits for them, and re-layouts  15.4 us (1%)
  between operations  14.2 us (1%)
    all_gather x1, waiting for transfers between devices, body(): query_sets = lax.all_gather(layer_groups[0], 'dp', axis=1, tiled=True)  375 us
    all_gather x1, waiting for transfers between devices, body(): output_full = lax.all_gather(layer_groups[1][0], 'dp', axis=1, tiled=True)  362 us
    all_gather x3, waiting for transfers between devices, run_layer(): gathered = lax.all_gather(incoming_state, 'tensor', axis=1, tiled=True)  74.7 us
    psum x3, blocking collectives, run_layer(): output_rank_state = lax.psum(rank_part, 'tensor').astype(jnp.bfloat16)  48.4 us
    dot_general x3, matrix products, output_pieces(): jnp.dot(attention_result, output_full, preferred_element_type=jnp.float32)  44.1 us
    dot_general x3, matrix products, run_layer(): jnp.dot(normed_state, query_matrix, preferred_element_type=jnp.float32)  43.5 us
    all_gather x3, blocking collectives, run_layer(): query_rank_state = lax.all_gather(rank_local, 'tensor', axis=1, tiled=True)  30.9 us
    reduce_scatter x3, waiting for transfers between devices, run_layer(): lax.psum_scatter(output_pieces(attention_result).astype(jnp.bfloat16), 't...  22.2 us
  transfers between devices with their start and end apart: 11, of which 10 were waited for; matrix products, arithmetic and copies ran while one was open for 5% of the time, Pallas kernels for 0%

commit v1 on v0

--- a/solution.py
+++ b/solution.py
@@ -1,6 +1,10 @@
+import functools
+
 import jax
 import jax.numpy as jnp
 from jax import lax
+from jax.experimental import pallas as pl
+from jax.experimental.pallas import tpu as pltpu
 from jax.sharding import PartitionSpec as P
 
 EPSILON = 1e-05
@@ -181,24 +185,485 @@
     return result
 
 
+MESH = pl.DeviceIdType.MESH
+
+
+def comm_call(kernel, outs, scratch, collective_id, *args):
+    vmem = pl.BlockSpec(memory_space=pltpu.VMEM)
+    return pl.pallas_call(
+        kernel,
+        out_shape=outs,
+        in_specs=[vmem] * len(args),
+        out_specs=jax.tree.map(lambda _: vmem, outs),
+        scratch_shapes=scratch,
+        compiler_params=pltpu.CompilerParams(
+            collective_id=collective_id, has_side_effects=True, vmem_limit_bytes=48 * 2**20
+        ),
+    )(*args)
+
+
+def greet(*targets):
+    barrier = pltpu.get_barrier_semaphore()
+    for target in targets:
+        pl.semaphore_signal(barrier, inc=1, device_id=target, device_id_type=MESH)
+    pl.semaphore_wait(barrier, len(targets))
+
+
+def remote(src, dst, send, recv, target):
+    return pltpu.make_async_remote_copy(
+        src_ref=src, dst_ref=dst, send_sem=send, recv_sem=recv, device_id=target, device_id_type=MESH
+    )
+
+
+def z_neighbours(k, tensor):
+    return [{"tensor": j} for j in (k - 1, k + 1) if 0 <= j < tensor]
+
+
+def gather_kernel(active, tensor, chunks, h_ref, own_ref, other_ref, zs, zr, xs, xr):
+    d, t, p = lax.axis_index("dp"), lax.axis_index("tensor"), lax.axis_index("pipe")
+    rows = h_ref.shape[0] // chunks
+    half = tensor // 2
+
+    @pl.when(p == active)
+    def _():
+        for k in range(tensor):
+
+            @pl.when(t == k)
+            def _(k=k):
+                greet({"dp": 1 - d}, *z_neighbours(k, tensor))
+                order = sorted(range(tensor), key=lambda s: abs(s - k))
+
+                def hop(s, c, dest):
+                    part = pl.ds(c * rows, rows)
+                    src = h_ref.at[part] if s == k else own_ref.at[s, part]
+                    way = 0 if dest > k else 1
+                    return remote(
+                        src, own_ref.at[s, part], zs.at[way, s, c], zr.at[s, c], {"tensor": dest}
+                    )
+
+                def across(s, c):
+                    part = pl.ds(c * rows, rows)
+                    src = h_ref.at[part] if s == k else own_ref.at[s, part]
+                    return remote(
+                        src, other_ref.at[s % half, part], xs.at[s, c], xr.at[s % half, c], {"dp": 1 - d}
+                    )
+
+                def arrived(s, c):
+                    part = pl.ds(c * rows, rows)
+                    view = own_ref.at[s, part]
+                    remote(view, view, zs.at[0, s, c], zr.at[s, c], {"dp": 1 - d}).wait_recv()
+
+                def dests(s):
+                    up = [k + 1] if s <= k and k + 1 < tensor else []
+                    down = [k - 1] if s >= k and k > 0 else []
+                    return up + down
+
+                for s in order:
+                    for c in range(chunks):
+                        if s != k:
+                            arrived(s, c)
+                        for dest in dests(s):
+                            hop(s, c, dest).start()
+
+                        @pl.when(s // half != d)
+                        def _(s=s, c=c):
+                            across(s, c).start()
+                    if s == k:
+                        own_ref[k] = h_ref[...]
+                for s in range(tensor):
+                    for c in range(chunks):
+                        for dest in dests(s):
+                            hop(s, c, dest).wait_send()
+
+                        @pl.when(s // half != d)
+                        def _(s=s, c=c):
+                            across(s, c).wait_send()
+                for j in range(half):
+                    for c in range(chunks):
+                        view = other_ref.at[j, pl.ds(c * rows, rows)]
+                        remote(view, view, xs.at[j, c], xr.at[j, c], {"dp": 1 - d}).wait_recv()
+
+
+def gather_rows(h, active, collective_id, tensor):
+    rows, cols = h.shape
+    chunks = 4
+    dma = pltpu.SemaphoreType.DMA
+    return comm_call(
+        functools.partial(gather_kernel, active, tensor, chunks),
+        (
+            jax.ShapeDtypeStruct((tensor, rows, cols), h.dtype),
+            jax.ShapeDtypeStruct((tensor // 2, rows, cols), h.dtype),
+        ),
+        [dma((2, tensor, chunks)), dma((tensor, chunks)), dma((tensor, chunks)), dma((tensor // 2, chunks))],
+        collective_id,
+        h,
+    )
+
+
+def exchange_kernel(active, tensor, blk_ref, small_ref, rblk_ref, rsmall_ref, bs, br, ss, sr):
+    d, t, p = lax.axis_index("dp"), lax.axis_index("tensor"), lax.axis_index("pipe")
+    count = 2 * tensor
+    me = d * tensor + t
+
+    def place(off):
+        target = lax.rem(me + off, count)
+        return target // tensor, lax.rem(target, tensor)
+
+    @pl.when(p == active)
+    def _():
+        greet(*[{"dp": place(off)[0], "tensor": place(off)[1]} for off in range(1, count)])
+        big = remote(blk_ref, rblk_ref, bs, br, {"dp": 1 - d})
+        copies = []
+        for off in range(1, count):
+            d2, t2 = place(off)
+            copies.append(
+                remote(
+                    small_ref.at[d2],
+                    rsmall_ref.at[d, t],
+                    ss.at[off],
+                    sr.at[off],
+                    {"dp": d2, "tensor": t2},
+                )
+            )
+        for copy in copies:
+            copy.start()
+        big.start()
+        rsmall_ref[d, t] = small_ref[d]
+        for copy in copies:
+            copy.wait()
+        big.wait()
+
+
+def exchange(block, small, active, collective_id, tensor):
+    dma = pltpu.SemaphoreType.DMA
+    return comm_call(
+        functools.partial(exchange_kernel, active, tensor),
+        (
+            jax.ShapeDtypeStruct(block.shape, block.dtype),
+            jax.ShapeDtypeStruct((2, tensor) + small.shape[1:], small.dtype),
+        ),
+        [dma, dma, dma((2 * tensor,)), dma((2 * tensor,))],
+        collective_id,
+        block,
+        small,
+    )
+
+
+def reduce_kernel(active, tensor, p_ref, h_ref, out_ref, up, dn, su, sd, us, ur, ds, dr, cs, cr):
+    t, p = lax.axis_index("tensor"), lax.axis_index("pipe")
+    chunks = p_ref.shape[0]
+
+    def to_core(c):
+        return remote(out_ref.at[c], out_ref.at[c], cs.at[c], cr.at[c], {"pipe": 1 - p})
+
+    @pl.when(p != active)
+    def _():
+        greet({"pipe": 1 - p})
+        for c in range(chunks):
+            to_core(c).wait_recv()
+
+    @pl.when(p == active)
+    def _():
+        for k in range(tensor):
+
+            @pl.when(t == k)
+            def _(k=k):
+                greet({"pipe": 1 - p}, *z_neighbours(k, tensor))
+                last = tensor - 1
+
+                def send_up(c, src):
+                    return remote(src.at[c], up.at[c], us.at[c], ur.at[c], {"tensor": k + 1})
+
+                def send_dn(c, src):
+                    return remote(src.at[c], dn.at[c], ds.at[c], dr.at[c], {"tensor": k - 1})
+
+                def f32(ref, c):
+                    return ref[c].astype(jnp.float32)
+
+                def up_step(c):
+                    remote(up.at[c], up.at[c], us.at[c], ur.at[c], {"pipe": 1 - p}).wait_recv()
+                    if k < last:
+                        su[c] = (f32(p_ref, c) + f32(up, c)).astype(su.dtype)
+                        send_up(c, su).start()
+
+                def dn_step(c):
+                    remote(dn.at[c], dn.at[c], ds.at[c], dr.at[c], {"pipe": 1 - p}).wait_recv()
+                    if k > 0:
+                        sd[c] = (f32(p_ref, c) + f32(dn, c)).astype(sd.dtype)
+                        send_dn(c, sd).start()
+
+                def finish(c):
+                    total = f32(h_ref, c) + f32(p_ref, c)
+                    if k > 0:
+                        total = total + f32(up, c)
+                    if k < last:
+                        total = total + f32(dn, c)
+                    out_ref[c] = total.astype(out_ref.dtype)
+                    to_core(c).start()
+
+                lag_up = max(0, 2 * k - last) if 0 < k < last else 0
+                lag_dn = max(0, last - 2 * k) if 0 < k < last else 0
+
+                if k == 0 or k == last:
+
+                    @pl.loop(0, chunks)
+                    def _(c):
+                        (send_up if k == 0 else send_dn)(c, p_ref).start()
+
+                for i in range(chunks + max(lag_up, lag_dn)):
+                    cu, cd = i - lag_up, i - lag_dn
+                    if k > 0 and 0 <= cu < chunks:
+                        up_step(cu)
+                    if k < last and 0 <= cd < chunks:
+                        dn_step(cd)
+                    done = i - max(lag_up, lag_dn)
+                    if done >= 0:
+                        finish(done)
+
+                @pl.loop(0, chunks)
+                def _(c):
+                    if k < last:
+                        send_up(c, p_ref if k == 0 else su).wait_send()
+                    if k > 0:
+                        send_dn(c, p_ref if k == last else sd).wait_send()
+                    to_core(c).wait_send()
+
+
+def reduce_rows(partial, h, active, collective_id, tensor):
+    rows, cols = partial.shape
+    chunks = 16
+    shape = (chunks, rows // chunks, cols)
+    dma = pltpu.SemaphoreType.DMA((chunks,))
+    buffer = pltpu.VMEM(shape, partial.dtype)
+    return comm_call(
+        functools.partial(reduce_kernel, active, tensor),
+        jax.ShapeDtypeStruct(shape, partial.dtype),
+        [buffer] * 4 + [dma] * 6,
+        collective_id,
+        partial.reshape(shape),
+        h.reshape(shape),
+    ).reshape(rows, cols)
+
+
+def scatter_kernel(
+    active, tensor, p_ref, out_ref, xb, up, dn, su, sd, res, xs, xr, us, ur, ds, dr, cs, cr
+):
+    d, t, p = lax.axis_index("dp"), lax.axis_index("tensor"), lax.axis_index("pipe")
+    half, chunks = p_ref.shape[1], p_ref.shape[2]
+    mine = chunks // 2
+    last = tensor - 1
+
+    def core_copy(c):
+        return remote(res.at[c], out_ref.at[c], cs.at[c], cr.at[c], {"pipe": 1 - p})
+
+    @pl.when(p != active)
+    def _():
+        greet({"pipe": 1 - p})
+        for c in range(mine):
+            core_copy(c).wait_recv()
+
+    @pl.when(p == active)
+    def _():
+        for k in range(tensor):
+
+            @pl.when(t == k)
+            def _(k=k):
+                greet({"pipe": 1 - p}, {"dp": 1 - d}, *z_neighbours(k, tensor))
+
+                def cross(j, c):
+                    return remote(
+                        p_ref.at[1 - d, j, c], xb.at[j, c], xs.at[j, c], xr.at[j, c], {"dp": 1 - d}
+                    )
+
+                def send_up(s, c):
+                    return remote(su.at[s, c], up.at[s, c], us.at[s, c], ur.at[s, c], {"tensor": k + 1})
+
+                def send_dn(s, c):
+                    return remote(sd.at[s, c], dn.at[s, c], ds.at[s, c], dr.at[s, c], {"tensor": k - 1})
+
+                def own(s, c):
+                    return jnp.where(
+                        d == s // half, p_ref[d, s % half, c], xb[s % half, c]
+                    ).astype(jnp.float32)
+
+                for c in range(chunks):
+                    for j in range(half):
+                        cross(j, c).start()
+
+                for c in range(chunks):
+                    for j in range(half):
+                        cross(j, c).wait_recv()
+                    for s in range(last, k, -1):
+                        total = own(s, c)
+                        if k > 0:
+                            send_up(s, c).wait_recv()
+                            total = total + up[s, c].astype(jnp.float32)
+                        su[s, c] = total.astype(su.dtype)
+                        send_up(s, c).start()
+                    for s in range(k):
+                        total = own(s, c)
+                        if k < last:
+                            send_dn(s, c).wait_recv()
+                            total = total + dn[s, c].astype(jnp.float32)
+                        sd[s, c] = total.astype(sd.dtype)
+                        send_dn(s, c).start()
+                for c in range(chunks):
+                    total = own(k, c)
+                    if k > 0:
+                        send_up(k, c).wait_recv()
+                        total = total + up[k, c].astype(jnp.float32)
+                    if k < last:
+                        send_dn(k, c).wait_recv()
+                        total = total + dn[k, c].astype(jnp.float32)
+                    if c < mine:
+                        res[c] = total.astype(res.dtype)
+                        core_copy(c).start()
+                    else:
+                        out_ref[c - mine] = total.astype(out_ref.dtype)
+                for c in range(chunks):
+                    for j in range(half):
+                        cross(j, c).wait_send()
+                    for s in range(k + 1, tensor):
+                        send_up(s, c).wait_send()
+                    for s in range(k):
+                        send_dn(s, c).wait_send()
+                for c in range(mine):
+                    core_copy(c).wait_send()
+
+
+def scatter_rows(partial, active, collective_id, tensor):
+    _, rows, half, cols = partial.shape
+    chunks = 4
+    part = rows // chunks
+    blocks = jnp.transpose(partial.reshape(2, chunks, part, half, cols), (0, 3, 1, 2, 4))
+    dma = pltpu.SemaphoreType.DMA
+    line = pltpu.VMEM((tensor, chunks, part, cols), partial.dtype)
+    return comm_call(
+        functools.partial(scatter_kernel, active, tensor),
+        jax.ShapeDtypeStruct((chunks // 2, part, cols), partial.dtype),
+        [pltpu.VMEM((half, chunks, part, cols), partial.dtype)]
+        + [line] * 4
+        + [pltpu.VMEM((chunks // 2, part, cols), partial.dtype)]
+        + [dma((half, chunks))] * 2
+        + [dma((tensor, chunks))] * 4
+        + [dma((chunks // 2,))] * 2,
+        collective_id,
+        blocks,
+    ).reshape(rows // 2, cols)
+
+
+def fast_layer(act, gain, weights, adapter_index, lengths, cache, newest, active, ids, tensor):
+    wq, wo, q_down, q_up, o_down, o_up = weights
+    d, t = lax.axis_index("dp"), lax.axis_index("tensor")
+    rows, k_half = act.shape[1:]
+    adapters, rank = q_up.shape[0], q_up.shape[1]
+    rank_local = q_down.shape[2]
+    head_dim, slots = cache.shape[-1] // 2, cache.shape[1]
+    features = k_half * 2
+
+    act32 = act.astype(jnp.float32)
+    gain_half = lax.dynamic_slice_in_dim(gain, d * k_half, k_half, 0)
+    scaled = (act32 * gain_half).astype(jnp.bfloat16).reshape(2 * rows, k_half)
+    squares = jnp.sum(act32 * act32, axis=-1)
+    partial = jnp.dot(scaled, wq, preferred_element_type=jnp.float32).reshape(2, rows, -1)
+    down_half = lax.dynamic_slice_in_dim(q_down, d * k_half, k_half, 1)
+    ranks = jnp.einsum("nk,akr->arn", scaled, down_half, preferred_element_type=jnp.float32)
+    ranks = jnp.transpose(ranks.reshape(adapters * rank_local, 2, rows), (1, 0, 2))
+    index_row = jnp.broadcast_to(adapter_index.astype(jnp.float32), (2, 1, rows))
+    small = jnp.concatenate([ranks, squares[:, None], index_row], axis=1)
+    small = jnp.pad(small, ((0, 0), (0, -small.shape[1] % 8), (0, 0)))
+    sent = lax.dynamic_index_in_dim(partial, 1 - d, 0, keepdims=False).astype(jnp.bfloat16)
+    came, smalls = exchange(sent, small, active, ids[0], tensor)
+    own = lax.dynamic_index_in_dim(partial, d, 0, keepdims=False)
+    width = adapters * rank_local
+    squares_all = smalls[0, 0, width] + smalls[1, 0, width]
+    factor = lax.rsqrt(squares_all / features + EPSILON)
+    selector = (adapter_index[:, None] == jnp.arange(adapters, dtype=jnp.int32)[None, :]).astype(jnp.float32)
+    rank_sum = (smalls[0, :, :width] + smalls[1, :, :width]).reshape(tensor, adapters, rank_local, rows)
+    rank_vec = jnp.einsum("tarn,na->ntr", rank_sum, selector * factor[:, None], precision=lax.Precision.HIGHEST)
+    rank_vec = rank_vec.reshape(rows, rank).astype(jnp.bfloat16)
+    query = (own + came.astype(jnp.float32)) * factor[:, None] + ADAPTER_SCALE * jnp.dot(
+        widen_rank(selector, rank_vec),
+        q_up.reshape(adapters * rank, -1),
+        preferred_element_type=jnp.float32,
+    )
+    query = query.astype(jnp.bfloat16).reshape(rows, slots, -1, head_dim)
+    attended = attend(query, cache, newest, lengths).reshape(rows, -1)
+
+    rank_every = jnp.einsum("cb,dbm->cdm", attended, o_down, preferred_element_type=jnp.float32)
+    rank_part = jnp.sum(selector[:, :, None] * rank_every, axis=1).T
+    came, rank_parts = exchange(
+        attended, jnp.broadcast_to(rank_part, (2,) + rank_part.shape), active, ids[1], tensor
+    )
+    first = jnp.where(d == 0, attended, came)
+    second = jnp.where(d == 0, came, attended)
+    both = jnp.concatenate([first, second], axis=0)
+    partial = jnp.dot(both, wo, preferred_element_type=jnp.float32)
+    rank_all = jnp.transpose(jnp.sum(rank_parts, axis=1), (0, 2, 1)).reshape(2 * rows, rank).astype(jnp.bfloat16)
+    index_all = smalls[:, 0, width + 1].reshape(2 * rows)
+    selector_all = (index_all[:, None] == jnp.arange(adapters, dtype=jnp.float32)[None, :]).astype(jnp.float32)
+    delta = ADAPTER_SCALE * jnp.dot(
+        widen_rank(selector_all, rank_all), o_up.reshape(adapters * rank, -1), preferred_element_type=jnp.float32
+    )
+    return partial.reshape(2 * rows, tensor // 2, -1), delta
+
+
+def fast_body(
+    residual_input, norm_gain, wq, wo, q_down, q_up, o_down, o_up, cache, newest, adapter_index, lengths
+):
+    tensor = lax.axis_size("tensor")
+    half = tensor // 2
+    d, t, p = lax.axis_index("dp"), lax.axis_index("tensor"), lax.axis_index("pipe")
+    rows, cols = residual_input.shape
+    weights = tuple(w[0] for w in (wq, wo, q_down, q_up, o_down, o_up))
+    gain = lax.dynamic_index_in_dim(norm_gain, p, 0, keepdims=False)
+    here = (jnp.arange(half) + d * half == t)[None, :, None]
+
+    own, other = gather_rows(residual_input, 0, 0, tensor)
+    mine = lax.dynamic_slice_in_dim(own, d * half, half, 0)
+    first = jnp.where(d == 0, mine, other)
+    second = jnp.where(d == 0, other, mine)
+    act = jnp.transpose(jnp.stack([first, second]), (0, 2, 1, 3)).reshape(2, rows, half * cols)
+
+    def layer(act, active, ids):
+        return fast_layer(
+            act, gain, weights, adapter_index, lengths, cache[0], newest[0], active, ids, tensor
+        )
+
+    partial, delta = layer(act, 0, (1, 2))
+    partial = jnp.where(here, partial + delta[:, None, :], partial).astype(jnp.bfloat16)
+    act = reduce_rows(
+        partial.reshape(2 * rows, half * cols), act.reshape(2 * rows, half * cols), 0, 3, tensor
+    )
+    act = act.reshape(2, rows, half * cols)
+    partial, delta = layer(act, 1, (4, 5))
+    residual = act.reshape(2 * rows, half, cols).astype(jnp.float32)
+    partial = jnp.where(here, partial + delta[:, None, :] + residual, partial).astype(jnp.bfloat16)
+    return scatter_rows(partial.reshape(2, rows, half, cols), 1, 6, tensor)
+
+
+SPECS = (
+    P(("groups", "dp"), "tensor"),
+    P(),
+    P("pipe", "dp", "tensor"),
+    P("pipe", "tensor", "dp"),
+    P("pipe", None, None, "tensor"),
+    P("pipe", None, None, "tensor"),
+    P("pipe", None, "tensor", None),
+    P("pipe", None, None, "tensor"),
+    P("pipe", ("groups", "dp"), "tensor", None, None),
+    P("pipe", ("groups", "dp"), "tensor", None),
+    P(("groups", "dp")),
+    P(("groups", "dp")),
+)
+
+
 def solution(mesh):
+    small = mesh.shape["dp"] == 2 and mesh.shape["tensor"] == 4 and mesh.shape["pipe"] == 2
     return jax.shard_map(
-        body,
+        fast_body if small else body,
         mesh=mesh,
-        in_specs=(
-            P(("groups", "dp"), "tensor"),
-            P(),
-            P("pipe", "dp", "tensor"),
-            P("pipe", "tensor", "dp"),
-            P("pipe", None, None, "tensor"),
-            P("pipe", None, None, "tensor"),
-            P("pipe", None, "tensor", None),
-            P("pipe", None, None, "tensor"),
-            P("pipe", ("groups", "dp"), "tensor", None, None),
-            P("pipe", ("groups", "dp"), "tensor", None),
-            P(("groups", "dp")),
-            P(("groups", "dp")),
-        ),
+        in_specs=SPECS,
         out_specs=P(("groups", "dp", "pipe"), "tensor"),
         check_vma=False,
     )

time: 1100 us -> 332 us (0.30)
  waiting for transfers between devices: 839 us -> 0 us
  Pallas kernels: 0 us -> 184 us
  blocking collectives: 79.4 us -> 0 us
  matrix products: 123 us -> 58.4 us
  local copies, waits for them, and re-layouts: 15.4 us -> 68.3 us
  between operations: 14.2 us -> 1.19 us
    all_gather x5 -> x0, waiting for transfers between devices: 811 us -> none  [the longest x1 375 us: body(): query_sets = lax.all_gather(layer_groups[0], 'dp', axis=1, tiled=True)]
    pallas_call x0 -> x7, Pallas kernels: none -> 184 us  [comm_call(): pl.pallas_call(kernel, out_shape=outs, in_specs=[vmem] * len(args), out_s...]
    dot_general x15 -> x10, matrix products: 103 us -> 45.9 us  [the longest x2 19.5 us: fast_layer(): partial = jnp.dot(both, wo, preferred_element_type=jnp.float32)]
    psum x3 -> x0, blocking collectives: 48.4 us -> none  [run_layer(): output_rank_state = lax.psum(rank_part, 'tensor').astype(jnp.bfloat16)]
    all_gather x3 -> x0, blocking collectives: 30.9 us -> none  [run_layer(): query_rank_state = lax.all_gather(rank_local, 'tensor', axis=1, tiled=True)]
    dot_general x0 -> x1, local copies, waits for them, and re-layouts: none -> 22.5 us  [fast_layer(): partial = jnp.dot(both, wo, preferred_element_type=jnp.float32)]
    reduce_scatter x3 -> x0, waiting for transfers between devices: 22.2 us -> none  [run_layer(): lax.psum_scatter(output_pieces(attention_result).astype(jnp.bfloat16), 't...]
    convert_element_type x15 -> x5, local copies, waits for them, and re-layouts: 1.65 us -> 14.2 us  [the longest x1 6.58 us: fast_body(): residual = act.reshape(2 * rows, half, cols).astype(jnp.float32)]
  transfers between devices with their start and end apart: 11 -> 0, of which waited for: 10 -> 0; matrix products, arithmetic and copies ran while one was open for 5% -> 0% of each run, Pallas kernels for 0% -> 0%
where the time goes in v1:
time: 332 us; the launch traced here: 330 us
  Pallas kernels  184 us (55%)
  local copies, waits for them, and re-layouts  68.3 us (21%)
  matrix products  58.4 us (18%)
  other arithmetic  17.7 us (5%)
    pallas_call x7, Pallas kernels, comm_call(): pl.pallas_call(kernel, out_shape=outs, in_specs=[vmem] * len(args), out_s...  184 us
    dot_general x1, local copies, waits for them, and re-layouts, fast_layer(): partial = jnp.dot(both, wo, preferred_element_type=jnp.float32)  22.5 us
    dot_general x2, matrix products, fast_layer(): partial = jnp.dot(both, wo, preferred_element_type=jnp.float32)  19.5 us
    dot_general x2, matrix products, fast_layer(): jnp.dot(scaled, wq, preferred_element_type=jnp.float32).reshape(2, rows, -1)  16.4 us
    unnamed x71, local copies, waits for them, and re-layouts  6.79 us

profile of v1, /device:TPU:1, one launch (start us, length us, event | category | flops | bytes accessed | tf_op | source)
XLA Modules:
  0.0 329.8 jit_solution(5828303780451908581)
XLA Ops:
  9.1 2.3 constant_dynamic-slice_fusion
  12.2 2.2 fusion.5
  14.5 3.5 %copy.75 = bf16[2,128,2,2048]{3,2,1,0:T(2,128)(2,1)} copy(bf16[2,128,2,2048]{3,1,2,0:T(8,128)(2,1)S(1)} %maximum_bitcast_fusion) | data formatting | bytes 4194304 | tf_op jit(solution)/shard_map/transpose | solution.py:626
  18.0 4.5 %reshape_reshape_reshape.4.h_ref = bf16[16,16,4096]{2,1,0:T(8,128)(2,1)} reshape(bf16[2,128,2,2048]{3,2,1,0:T(2,128)(2,1)} %copy.75) | data formatting | bytes 4194304 | tf_op jit(solution)/shard_map/reshape;reshape;reshape | solution.py:444
  22.5 4.0 %copy.64 = bf16[2,128,2,2048]{1,3,2,0:T(8,128)(2,1)} copy(bf16[2,128,2,2048]{3,1,2,0:T(8,128)(2,1)} %get-tuple-element.32) | data formatting | bytes 4194304 | tf_op jit(solution)/shard_map/convert_element_type | solution.py:566
  26.5 2.2 convolution_bitcast_fusion.1
  28.7 8.2 %fusion.2 = f32[2,128,2048]{2,1,0:T(8,128)S(1)} fusion(bf16[2,128,4096]{1,2,0:T(8,128)(2,1)S(1)} %bitcast.202, bf16[1,4096,2048]{2,1,0:T(8,128)(2,1)} %param.14), kind=kOutput, calls=%fused_computation.2 | convolution fusion | flops 4294967296 | bytes 20971520 | tf_op jit(solution)/shard_map/dot_general | solution.py:568
  37.1 12.1 %shard_map.119 = (bf16[128,2048]{1,0:T(8,128)(2,1)S(1)}, f32[2,4,136,128]{3,2,1,0:T(8,128)S(1)}) custom-call(bf16[128,2048]{1,0:T(8,128)(2,1)S(1)} %fusion.29.blk_ref, f32[2,136,128]{2,1,0:T(8,128)S(1)} %pad.7.small_ref), custom_call_target="tpu_custom_call" | custom-call | tf_op jit(solution)/shard_map/pallas_call | solution.py:193
  52.1 3.1 select_reduce_fusion.1
  62.3 2.6 fusion.13
  69.3 22.5 %copy.100 = bf16[4096,2048]{1,0:T(8,128)(2,1)} copy(bf16[4096,2048]{0,1:T(8,128)(2,1)} %bitcast.203) | data formatting | bytes 33554432 | tf_op jit(solution)/shard_map/dot_general | solution.py:601
  91.8 9.0 %fusion.6 = bf16[256,2,2048]{2,0,1:T(8,128)(2,1)S(1)} fusion(bf16[2,2048,2048]{2,1,0:T(8,128)(2,1)} %bitcast.204, f32[256,2048]{1,0:T(8,128)} %convolution_multiply_fusion.1, pred[2]{0:T(512)(128)(4,1)S(1)} %copy-done.31, bf16[128,2048]{1,0:T(8,128)(2,1)} %get-tuple-element.36, bf16[128,2048]{1,0:T(8,128)(2,1)} %get-tuple-element.35), kind=kOutput, calls=%fused_computation.9 | convolution fusion | flops 4300210176 | bytes 22020098 | tf_op jit(solution)/shard_map/dot_general | solution.py:601
  100.8 3.5 %copy.74 = bf16[256,2,2048]{2,1,0:T(2,128)(2,1)} copy(bf16[256,2,2048]{2,0,1:T(8,128)(2,1)S(1)} %fusion.6) | data formatting | bytes 4194304 | tf_op jit(solution)/shard_map/convert_element_type | solution.py:634
  104.3 4.5 %reshape_reshape.7.p_ref = bf16[16,16,4096]{2,1,0:T(8,128)(2,1)} reshape(bf16[256,2,2048]{2,1,0:T(2,128)(2,1)} %copy.74) | data formatting | bytes 4194304 | tf_op jit(solution)/shard_map/reshape;reshape | solution.py:443
  110.3 109.9 %shard_map.121 = bf16[16,16,4096]{2,1,0:T(8,128)(2,1)S(1)} custom-call(bf16[16,16,4096]{2,1,0:T(8,128)(2,1)S(1)} %copy-done.2, bf16[16,16,4096]{2,1,0:T(8,128)(2,1)} %reshape_reshape_reshape.4.h_ref), custom_call_target="tpu_custom_call" | custom-call | tf_op jit(solution)/shard_map/pallas_call | solution.py:193
  222.4 2.6 convolution_bitcast_fusion
  225.0 8.2 %fusion = f32[2,128,2048]{2,1,0:T(8,128)S(1)} fusion(bf16[2,128,4096]{2,1,0:T(8,128)(2,1)S(1)} %bitcast.213, bf16[1,4096,2048]{2,1,0:T(8,128)(2,1)} %param.14), kind=kOutput, calls=%fused_computation | convolution fusion | flops 4294967296 | bytes 20971520 | tf_op jit(solution)/shard_map/dot_general | solution.py:568
  233.4 13.0 %shard_map.122 = (bf16[128,2048]{1,0:T(8,128)(2,1)S(1)}, f32[2,4,136,128]{3,2,1,0:T(8,128)S(1)}) custom-call(bf16[128,2048]{1,0:T(8,128)(2,1)S(1)} %fusion.30.blk_ref, f32[2,136,128]{2,1,0:T(8,128)S(1)} %pad.8.small_ref), custom_call_target="tpu_custom_call" | custom-call | tf_op jit(solution)/shard_map/pallas_call | solution.py:193
  249.2 2.2 select_reduce_fusion
  257.5 2.3 fusion.14
  260.7 10.9 %shard_map.123 = (bf16[128,2048]{1,0:T(8,128)(2,1)S(1)}, f32[2,4,64,128]{3,2,1,0:T(8,128)S(1)}) custom-call(bf16[128,2048]{1,0:T(8,128)(2,1)S(1)} %bitcast.199, f32[2,64,128]{2,1,0:T(8,128)S(1)} %broadcast_in_dim.55.small_ref), custom_call_target="tpu_custom_call" | custom-call | tf_op jit(solution)/shard_map/pallas_call | solution.py:193
  273.9 6.6 %reshape.334 = f32[256,2,2048]{2,1,0:T(2,128)} reshape(bf16[16,16,4096]{2,1,0:T(8,128)(2,1)} %copy-done.1) | data formatting | bytes 6291456 | tf_op jit(solution)/shard_map/convert_element_type | solution.py:640
  280.5 10.5 %fusion.8 = bf16[256,2,2048]{2,0,1:T(8,128)(2,1)S(1)} fusion(f32[256,2,2048]{2,1,0:T(2,128)} %reshape.334, bf16[2,2048,2048]{2,1,0:T(8,128)(2,1)} %bitcast.205, f32[256,2048]{1,0:T(8,128)} %convolution_multiply_fusion, pred[2]{0:T(512)(128)(4,1)S(1)} %copy-done.32, bf16[128,2048]{1,0:T(8,128)(2,1)S(1)} %get-tuple-element.34, ...), kind=kOutput, calls=%fused_computation.12 | convolution fusion | flops 4301258752 | bytes 26214402 | tf_op jit(solution)/shard_map/dot_general | solution.py:601
  291.1 37.5 %shard_map.124 = bf16[2,32,2048]{2,1,0:T(8,128)(2,1)S(1)} custom-call(bf16[2,2,4,32,2048]{4,3,2,1,0:T(8,128)(2,1)S(1)} %bitcast.197), custom_call_target="tpu_custom_call" | custom-call | tf_op jit(solution)/shard_map/pallas_call | solution.py:193
  (147 shorter events, 40.8 us)
Async XLA Ops:
  0.0 1.6 copy-start
  0.0 11.4 %copy-start.3 = (bf16[128,2048]{1,0:T(8,128)(2,1)S(1)}, bf16[128,2048]{1,0:T(8,128)(2,1)}, u32[]{:S(2)}) copy-start(bf16[128,2048]{1,0:T(8,128)(2,1)} %h_ref.1) | copy-start | bytes 1572868
  9.0 53.3 %copy-start.13 = (f32[128,2,128]{2,1,0:T(2,128)}, f32[128,2,128]{2,1,0:T(2,128)S(1)}, u32[]{:S(2)}) copy-start(f32[128,2,128]{2,1,0:T(2,128)S(1)} %get-tuple-element.38) | copy-start | bytes 393220
  22.5 4.0 %copy-start.5 = (bf16[1,8,4096,16]{2,3,1,0:T(8,128)(2,1)S(1)}, bf16[1,8,4096,16]{2,3,1,0:T(8,128)(2,1)}, u32[]{:S(2)}) copy-start(bf16[1,8,4096,16]{2,3,1,0:T(8,128)(2,1)} %constant_dynamic-slice_fusion) | copy-start | bytes 3145732
  26.5 2.2 copy-start.4
  28.7 8.2 %copy-start.29 = (f32[2,1,128]{2,1,0:T(1,128)S(1)}, f32[2,1,128]{2,1,0:T(1,128)}, u32[]{:S(2)}) copy-start(f32[2,1,128]{2,1,0:T(1,128)} %broadcast_in_dim.50) | copy-start | bytes 3076
  36.9 12.4 %copy-start.27 = (s32[128]{0:T(128)S(1)}, s32[128]{0:T(128)}, u32[]{:S(2)}) copy-start(s32[128]{0:T(128)} %param.22) | copy-start | bytes 1540
  36.9 13.0 %copy-start.15 = (f32[128,8]{0,1:T(8,128)S(1)}, f32[128,8]{0,1:T(8,128)}, u32[]{:S(2)}) copy-start(f32[128,8]{0,1:T(8,128)} %fusion.51) | copy-start | bytes 12292
  37.0 13.1 %copy-start.6 = (bf16[1,8,64,2048]{3,2,1,0:T(8,128)(2,1)S(1)}, bf16[1,8,64,2048]{3,2,1,0:T(8,128)(2,1)}, u32[]{:S(2)}) copy-start(bf16[1,8,64,2048]{3,2,1,0:T(8,128)(2,1)} %param.17) | copy-start | bytes 6291460
  52.1 3.2 copy-start.18
  62.3 2.6 copy-start.8
  69.3 22.5 %copy-start.31 = (pred[2]{0:T(512)(128)(4,1)S(1)}, pred[2]{0:T(512)(128)(4,1)}, u32[]{:S(2)}) copy-start(pred[2]{0:T(512)(128)(4,1)} %add_compare_fusion) | copy-start | bytes 10
  108.7 1.6 copy-start.2
  110.3 109.9 %copy-start.22 = (f32[1,4096]{1,0:T(1,128)S(1)}, f32[1,4096]{1,0:T(1,128)}, u32[]{:S(2)}) copy-start(f32[1,4096]{1,0:T(1,128)} %get-tuple-element.26) | copy-start | bytes 49156
  220.2 2.1 copy-start.1
  222.4 2.6 copy-start.10
  225.0 8.2 %copy-start.30 = (f32[2,1,128]{2,1,0:T(1,128)S(1)}, f32[2,1,128]{2,1,0:T(1,128)}, u32[]{:S(2)}) copy-start(f32[2,1,128]{2,1,0:T(1,128)} %broadcast_in_dim.50) | copy-start | bytes 3076
  233.2 13.3 %copy-start.28 = (s32[128]{0:T(128)S(1)}, s32[128]{0:T(128)}, u32[]{:S(2)}) copy-start(s32[128]{0:T(128)} %param.22) | copy-start | bytes 1540
  233.2 13.9 %copy-start.7 = (bf16[1,8,64,2048]{3,2,1,0:T(8,128)(2,1)S(1)}, bf16[1,8,64,2048]{3,2,1,0:T(8,128)(2,1)}, u32[]{:S(2)}) copy-start(bf16[1,8,64,2048]{3,2,1,0:T(8,128)(2,1)} %param.17) | copy-start | bytes 6291460
  249.2 2.3 copy-start.19
  249.2 8.2 %copy-start.14 = (f32[128,2,128]{2,1,0:T(2,128)S(1)}, f32[128,2,128]{2,1,0:T(2,128)}, u32[]{:S(2)}) copy-start(f32[128,2,128]{2,1,0:T(2,128)} %copy-done.13) | copy-start | bytes 393220
  257.5 2.3 copy-start.9
  260.5 11.2 %copy-start.25 = (f32[256,8]{0,1:T(8,128)S(1)}, f32[256,8]{0,1:T(8,128)}, u32[]{:S(2)}) copy-start(f32[256,8]{0,1:T(8,128)} %fusion.44) | copy-start | bytes 24580
  273.9 6.6 %copy-start.32 = (pred[2]{0:T(512)(128)(4,1)S(1)}, pred[2]{0:T(512)(128)(4,1)}, u32[]{:S(2)}) copy-start(pred[2]{0:T(512)(128)(4,1)} %add_compare_fusion) | copy-start | bytes 10
  (9 other events, 9.0 us)
